TPU v7x, 512 devices: a whole 4x4x16 slice. The times are simulated.
512 devices in a mesh: seq: 32 (over y_hi, z), head: 16 (over y_lo, x, core).
Axes of the slice: x: 4, y: 4 (y_hi: 2, y_lo: 2; y = y_hi * 2 + y_lo), z: 16, core: 2. Of those that a mesh axis runs over, the one named last changes fastest.
Arguments:
- queries: bfloat16 [8192, 6144], P('seq', 'head'), may hold values from -42 to 42
- keys: bfloat16 [8192, 6144], P('seq', 'head'), may hold values from -4 to 4
- values: bfloat16 [8192, 6144], P('seq', 'head'), may hold values from -120 to 120
- block_mask: int32 [64, 64], P('seq'), may hold values from 0 to 1
- region_of_block: int32 [64], P('seq'), may hold values from 0 to 7
- text_keys: bfloat16 [8, 256, 6144], P(None, 'seq', 'head'), may hold values from -4 to 4
- text_values: bfloat16 [8, 256, 6144], P(None, 'seq', 'head'), may hold values from -6 to 6
- gain: bfloat16 [6144], P('head'), may hold values from 0.099609375 to 1.8984375
Outputs:
- mixed: bfloat16 [8192, 6144], P('seq', 'head')
All inputs are finite; a program needn't handle non-finite values.
Results may differ from a plain program's by a relative error of at most 0.0085.
Values may be sent and summed in bfloat16 or wider, within the bound.
A program may use at most 64 MiB of HBM per device.

v0:
```python
import jax
import jax.numpy as jnp
from jax import lax
from jax.sharding import PartitionSpec as P

HEADS = 48
HD = 128
BLK = 128
TXT = 256


def absorb(carry, query_rows, key_block, value_block, tile, softmax_scale):
    top, total, accum = carry
    keep = jnp.repeat(jnp.repeat(tile, BLK, axis=0), BLK, axis=1)
    scores = (
        jnp.einsum("qhd,khd->hqk", query_rows, key_block, preferred_element_type=jnp.float32)
        * softmax_scale
    )
    scores = jnp.where(keep[None], scores, -1e30)
    new_top = jnp.maximum(top, jnp.max(scores, axis=-1))
    weights = jnp.where(keep[None], jnp.exp(scores - new_top[..., None]), 0.0)
    factor = jnp.exp(top - new_top)
    total = total * factor + jnp.sum(weights, axis=-1)
    update = jnp.einsum(
        "hqk,khd->hqd",
        weights.astype(jnp.bfloat16),
        value_block,
        preferred_element_type=jnp.float32,
    )
    accum = accum * factor[..., None] + update
    return (new_top, total, accum)


def local(queries, keys, values, block_mask, region_of_block, text_keys, text_values, gain):
    tok, width = queries.shape
    heads = width // HD
    blocks = tok // BLK
    softmax_scale = HD ** (-0.5)
    first = lax.axis_index("seq") * blocks
    columns = jnp.arange(block_mask.shape[1], dtype=jnp.int32)
    owned = first + jnp.arange(blocks, dtype=jnp.int32)
    allowed = (block_mask > 0) | (columns[None, :] == owned[:, None])
    query_rows = queries.reshape(tok, heads, HD)
    start_state = (
        jnp.full((heads, tok), -1e30, jnp.float32),
        jnp.zeros((heads, tok), jnp.float32),
        jnp.zeros((heads, tok, HD), jnp.float32),
    )
    key_piece = lax.all_gather(keys, "seq", axis=0, tiled=True)
    value_piece = lax.all_gather(values, "seq", axis=0, tiled=True)
    rows = key_piece.shape[0]
    stride = 2 * tok

    def inner(index, carry):
        offset = index * stride
        key_block = lax.dynamic_slice_in_dim(key_piece, offset, stride, 0).reshape(
            stride, heads, HD
        )
        value_block = lax.dynamic_slice_in_dim(value_piece, offset, stride, 0).reshape(
            stride, heads, HD
        )
        tile = lax.dynamic_slice_in_dim(allowed, offset // BLK, stride // BLK, 1)
        return absorb(carry, query_rows, key_block, value_block, tile, softmax_scale)

    state = lax.fori_loop(0, rows // stride, inner, start_state)
    region_panel_key_rows, region_panel_value_rows = (
        lax.all_gather(text_keys, "seq", axis=1, tiled=True),
        lax.all_gather(text_values, "seq", axis=1, tiled=True),
    )
    top, total, accum = state
    self_out = jnp.transpose(accum / total[..., None], (1, 0, 2)).reshape(tok, width)
    chosen_keys = region_panel_key_rows[region_of_block].reshape(blocks, TXT, heads, HD)
    chosen_values = region_panel_value_rows[region_of_block].reshape(blocks, TXT, heads, HD)
    query_block_groups = queries.reshape(blocks, BLK, heads, HD)
    caption_score_matrix = (
        jnp.einsum(
            "bqhd,bthd->bhqt", query_block_groups, chosen_keys, preferred_element_type=jnp.float32
        )
        * softmax_scale
    )
    text_top = jnp.max(caption_score_matrix, axis=-1, keepdims=True)
    text_weights = jnp.exp(caption_score_matrix - text_top)
    caption_score_sum = jnp.sum(text_weights, axis=-1)
    cross_sum = jnp.einsum(
        "bhqt,bthd->bqhd",
        text_weights.astype(jnp.bfloat16),
        chosen_values,
        preferred_element_type=jnp.float32,
    )
    cross_out = (cross_sum / jnp.transpose(caption_score_sum, (0, 2, 1))[..., None]).reshape(
        tok, width
    )
    combined = self_out + cross_out
    squares = jnp.sum(combined * combined, axis=1)
    square_total = lax.psum(squares, "head")
    mean_square = square_total / (HEADS * HD)
    scaled = combined * lax.rsqrt(mean_square + 1e-06)[:, None] * gain.astype(jnp.float32)[None, :]
    return scaled.astype(jnp.bfloat16)


def solution(mesh):
    in_specs = (
        P("seq", "head"),
        P("seq", "head"),
        P("seq", "head"),
        P("seq", None),
        P("seq"),
        P(None, "seq", "head"),
        P(None, "seq", "head"),
        P("head"),
    )
    out_specs = P("seq", "head")
    return jax.shard_map(local, mesh=mesh, in_specs=in_specs, out_specs=out_specs, check_vma=False)
```

profile of v0, /device:TPU:1, one launch (start us, length us, event | category | flops | bytes accessed | tf_op | source)
XLA Modules:
  0.0 747.4 jit_solution(13527715328726537299)
XLA Ops:
  8.1 1.7 copy.37
  9.9 1.7 copy.39
  13.2 133.5 %all-gather.11.cloned.1.call-done = bf16[8,256,384]{2,1,0:T(8,128)(2,1)} async-done(((bf16[8,8,384]{2,1,0:T(8,128)(2,1)}), bf16[8,256,384]{2,1,0:T(8,128)(2,1)}) %all-gather.11.cloned.1.call-update) | async-done | bytes 1572880 | tf_op jit(solution)/shard_map/all_gather | solution.py:67
  146.7 2.0 gather_fusion.1
  148.9 135.7 %all-gather.9.cloned.1.call-done = bf16[8,256,384]{2,1,0:T(8,128)(2,1)} async-done(((bf16[8,8,384]{2,1,0:T(8,128)(2,1)}), bf16[8,256,384]{2,1,0:T(8,128)(2,1)}) %all-gather.9.cloned.1.call-update) | async-done | bytes 1572880 | tf_op jit(solution)/shard_map/all_gather | solution.py:68
  284.6 2.0 gather_fusion
  288.1 183.3 %all-gather.5.cloned.1.call-done = bf16[8192,384]{0,1:T(8,128)(2,1)} async-done(((bf16[256,384]{0,1:T(8,128)(2,1)}), bf16[8192,384]{0,1:T(8,128)(2,1)}) %all-gather.5.cloned.1.call-update) | async-done | bytes 6291472 | tf_op jit(solution)/shard_map/all_gather | solution.py:49
  471.4 185.5 %all-gather.7.cloned.1.call-done = bf16[8192,384]{0,1:T(8,128)(2,1)} async-done(((bf16[256,384]{0,1:T(8,128)(2,1)}), bf16[8192,384]{0,1:T(8,128)(2,1)}) %all-gather.7.cloned.1.call-update) | async-done | bytes 6291472 | tf_op jit(solution)/shard_map/all_gather | solution.py:50
  656.8 46.9 %while.20 = (s32[]{:T(128)}, f32[3,256]{1,0:T(4,128)S(1)}, f32[3,256]{1,0:T(4,128)S(1)}, f32[3,256,128]{2,1,0:T(8,128)S(1)}, pred[2,64]{1,0:T(4,128)(4,1)S(1)}, ...) while((s32[]{:T(128)}, f32[3,256]{1,0:T(4,128)S(1)}, ...), condition=%wide.region_3.4_spmd.clone, body=%wide.region_0.3_spmd.clone.sunk | while | flops 205164320 | bytes 8636830 | solution.py:65
  657.0 1.2 constant_dynamic-slice_fusion.5
  660.0 1.2 constant_dynamic-slice_fusion.5
  662.9 1.2 constant_dynamic-slice_fusion.5
  665.9 1.2 constant_dynamic-slice_fusion.5
  668.8 1.2 constant_dynamic-slice_fusion.5
  671.7 1.2 constant_dynamic-slice_fusion.5
  674.7 1.2 constant_dynamic-slice_fusion.5
  677.6 1.2 constant_dynamic-slice_fusion.5
  680.5 1.2 constant_dynamic-slice_fusion.5
  683.5 1.2 constant_dynamic-slice_fusion.5
  686.4 1.2 constant_dynamic-slice_fusion.5
  689.3 1.2 constant_dynamic-slice_fusion.5
  698.1 1.2 constant_dynamic-slice_fusion.5
  701.1 1.2 constant_dynamic-slice_fusion.5
  704.0 35.9 %psum.7 = f32[256]{0:T(256)S(1)} all-reduce(f32[256]{0:T(256)S(1)} %get-tuple-element.268), channel_id=1, replica_groups=mesh['seq'=32,'head'=16] {'head'}, use_global_device_ids=true, to_apply=%region_7.8 | all-reduce | flops 256 | bytes 2048 | tf_op jit(solution)/shard_map/psum | solution.py:95
  (186 shorter events, 34.8 us)
Async XLA Ops:
  6.5 6.1 copy-start
  6.5 6.5 copy-start.1
  6.5 6.5 copy-start.3
  6.5 6.5 copy-start.2
  6.5 140.1 %all-gather.11.cloned.1.call-start = ((), (), s32[]{:S(2)}) async-start(), calls=%async_computation.3 | async-start | bytes 1622016 | tf_op jit(solution)/shard_map/all_gather | solution.py:67
  7.3 277.3 %all-gather.9.cloned.1.call-start = ((), (), s32[]{:S(2)}) async-start(), calls=%async_computation.2 | async-start | bytes 1622016 | tf_op jit(solution)/shard_map/all_gather | solution.py:68
  8.0 463.4 %all-gather.5.cloned.1.call-start = ((), (), s32[]{:S(2)}) async-start(), calls=%async_computation | async-start | bytes 6488064 | tf_op jit(solution)/shard_map/all_gather | solution.py:49
  9.8 647.0 %all-gather.7.cloned.1.call-start = ((), (), s32[]{:S(2)}) async-start(), calls=%async_computation.1 | async-start | bytes 6488064 | tf_op jit(solution)/shard_map/all_gather | solution.py:50
Sparse Core Ops, SparseCore 0:
  10.3 136.3 all-gather.10
  149.6 134.9 all-gather.8
  287.5 183.8 all-gather.4
  474.1 182.6 all-gather.6
where the time goes:
time: 748 us; the launch traced here: 747 us
  waiting for transfers between devices  639 us (85%)
  blocking collectives  35.9 us (5%)
  local copies, waits for them, and re-layouts  32.6 us (4%)
  matrix products  18.8 us (3%)
  between operations  13.3 us (2%)
    all_gather x1, waiting for transfers between devices, local(): value_piece = lax.all_gather(values, 'seq', axis=0, tiled=True)  185 us
    all_gather x1, waiting for transfers between devices, local(): key_piece = lax.all_gather(keys, 'seq', axis=0, tiled=True)  183 us
    all_gather x1, waiting for transfers between devices, local(): lax.all_gather(text_values, 'seq', axis=1, tiled=True)  136 us
    all_gather x1, waiting for transfers between devices, local(): lax.all_gather(text_keys, 'seq', axis=1, tiled=True)  134 us
    psum x1, blocking collectives, local(): square_total = lax.psum(squares, 'head')  35.9 us
    dynamic_slice x16, local copies, waits for them, and re-layouts, inner(): lax.dynamic_slice_in_dim(value_piece, offset, stride, 0)  18.8 us
  transfers between devices with their start and end apart: 4, of which 4 were waited for; matrix products, arithmetic and copies ran while one was open for 1% of the time, Pallas kernels for 0%

commit v1 on v0

--- a/solution.py
+++ b/solution.py
@@ -64,7 +64,9 @@
 
     state = lax.fori_loop(0, rows // stride, inner, start_state)
     region_panel_key_rows, region_panel_value_rows = (
-        lax.all_gather(text_keys, "seq", axis=1, tiled=True),
+        jnp.concatenate(
+            lax.all_to_all(jnp.stack([text_keys] * lax.axis_size("seq")), "seq", 0, 0), axis=1
+        ),
         lax.all_gather(text_values, "seq", axis=1, tiled=True),
     )
     top, total, accum = state

time: 748 us -> 646 us (0.86)
  waiting for transfers between devices: 639 us -> 516 us
  starting transfers between devices: 0.15 us -> 18.9 us
    all_gather x1 -> x0, waiting for transfers between devices: 134 us -> none  [local(): lax.all_gather(text_keys, 'seq', axis=1, tiled=True)]
    all_to_all x0 -> x1, starting transfers between devices: none -> 18.8 us  [local(): lax.all_to_all(jnp.stack([text_keys] * lax.axis_size('seq')), 'seq', 0, 0)]
    all_gather x1, waiting for transfers between devices: 136 us -> 150 us  [local(): lax.all_gather(text_values, 'seq', axis=1, tiled=True)]
  transfers between devices with their start and end apart: 4 -> 4, of which waited for: 4 -> 3; matrix products, arithmetic and copies ran while one was open for 1% -> 2% of each run, Pallas kernels for 0% -> 0%
where the time goes in v1:
time: 646 us
  waiting for transfers between devices  516 us (80%)
  blocking collectives  35.9 us (6%)
  local copies, waits for them, and re-layouts  35.2 us (5%)
  matrix products  19.1 us (3%)
  starting transfers between devices  18.9 us (3%)
  between operations  13.3 us (2%)
    all_gather x1, waiting for transfers between devices, local(): value_piece = lax.all_gather(values, 'seq', axis=0, tiled=True)  186 us
    all_gather x1, waiting for transfers between devices, local(): key_piece = lax.all_gather(keys, 'seq', axis=0, tiled=True)  180 us
    all_gather x1, waiting for transfers between devices, local(): lax.all_gather(text_values, 'seq', axis=1, tiled=True)  150 us
    psum x1, blocking collectives, local(): square_total = lax.psum(squares, 'head')  35.9 us
    dynamic_slice x16, local copies, waits for them, and re-layouts, inner(): lax.dynamic_slice_in_dim(value_piece, offset, stride, 0)  18.8 us
    all_to_all x1, starting transfers between devices, local(): lax.all_to_all(jnp.stack([text_keys] * lax.axis_size('seq')), 'seq', 0, 0)  18.8 us
  transfers between devices with their start and end apart: 4, of which 3 were waited for; matrix products, arithmetic and copies ran while one was open for 2% of the time, Pallas kernels for 0%

profile of v1, /device:TPU:1, one launch (start us, length us, event | category | flops | bytes accessed | tf_op | source)
XLA Modules:
  0.0 645.7 jit_solution(16096994445094133896)
XLA Ops:
  7.3 1.7 copy.56
  9.1 1.8 copy.58
  10.9 2.2 stack.2
  13.1 18.8 %all-to-all-start = ((bf16[32,8,8,384]{3,2,1,0:T(8,128)(2,1)}), bf16[32,8,8,384]{3,2,1,0:T(8,128)(2,1)S(1)}, u32[]{:S(2)}, u32[]{:S(2)}) async-start(bf16[32,8,8,384]{3,2,1,0:T(8,128)(2,1)} %stack.2), calls=%async_computation | async-start | bytes 3145728 | tf_op jit(solution)/shard_map/all_to_all | solution.py:68
  32.5 150.2 %all-gather.8.cloned.1.call-done = bf16[8,256,384]{2,1,0:T(8,128)(2,1)} async-done(((bf16[8,8,384]{2,1,0:T(8,128)(2,1)}), bf16[8,256,384]{2,1,0:T(8,128)(2,1)}) %all-gather.8.cloned.1.call-update) | async-done | bytes 1572880 | tf_op jit(solution)/shard_map/all_gather | solution.py:70
  182.7 2.0 gather_fusion
  184.9 1.4 copy.88
  186.3 2.0 gather_fusion.1
  189.8 179.7 %all-gather.4.cloned.1.call-done = bf16[8192,384]{0,1:T(8,128)(2,1)} async-done(((bf16[256,384]{0,1:T(8,128)(2,1)}), bf16[8192,384]{0,1:T(8,128)(2,1)}) %all-gather.4.cloned.1.call-update) | async-done | bytes 6291472 | tf_op jit(solution)/shard_map/all_gather | solution.py:49
  369.5 185.6 %all-gather.6.cloned.1.call-done = bf16[8192,384]{0,1:T(8,128)(2,1)} async-done(((bf16[256,384]{0,1:T(8,128)(2,1)}), bf16[8192,384]{0,1:T(8,128)(2,1)}) %all-gather.6.cloned.1.call-update) | async-done | bytes 6291472 | tf_op jit(solution)/shard_map/all_gather | solution.py:50
  555.1 47.0 %while.20 = (s32[]{:T(128)}, f32[3,256]{1,0:T(4,128)S(1)}, f32[3,256]{1,0:T(4,128)S(1)}, f32[3,256,128]{2,1,0:T(8,128)S(1)}, pred[2,64]{1,0:T(4,128)(4,1)S(1)}, ...) while((s32[]{:T(128)}, f32[3,256]{1,0:T(4,128)S(1)}, ...), condition=%wide.region_3.4_spmd.clone, body=%wide.region_0.3_spmd.clone.sunk | while | flops 205164320 | bytes 8636838 | solution.py:65
  555.3 1.2 constant_dynamic-slice_fusion.5
  558.2 1.2 constant_dynamic-slice_fusion.5
  561.1 1.2 constant_dynamic-slice_fusion.5
  564.1 1.2 constant_dynamic-slice_fusion.5
  567.0 1.2 constant_dynamic-slice_fusion.5
  570.0 1.2 constant_dynamic-slice_fusion.5
  572.9 1.2 constant_dynamic-slice_fusion.5
  575.9 1.2 constant_dynamic-slice_fusion.5
  578.8 1.2 constant_dynamic-slice_fusion.5
  581.7 1.2 constant_dynamic-slice_fusion.5
  584.7 1.2 constant_dynamic-slice_fusion.5
  587.6 1.2 constant_dynamic-slice_fusion.5
  602.4 35.9 %psum.7 = f32[256]{0:T(256)S(1)} all-reduce(f32[256]{0:T(256)S(1)} %get-tuple-element.276), channel_id=1, replica_groups=mesh['seq'=32,'head'=16] {'head'}, use_global_device_ids=true, to_apply=%region_7.8 | all-reduce | flops 256 | bytes 2048 | tf_op jit(solution)/shard_map/psum | solution.py:97
  (187 shorter events, 35.7 us)
Async XLA Ops:
  6.5 176.2 %all-gather.8.cloned.1.call-start = ((), (), s32[]{:S(2)}) async-start(), calls=%async_computation.3 | async-start | bytes 1622016 | tf_op jit(solution)/shard_map/all_gather | solution.py:70
  7.3 362.2 %all-gather.4.cloned.1.call-start = ((), (), s32[]{:S(2)}) async-start(), calls=%async_computation.1 | async-start | bytes 6488064 | tf_op jit(solution)/shard_map/all_gather | solution.py:49
  9.1 546.0 %all-gather.6.cloned.1.call-start = ((), (), s32[]{:S(2)}) async-start(), calls=%async_computation.2 | async-start | bytes 6488064 | tf_op jit(solution)/shard_map/all_gather | solution.py:50
  13.1 18.8 %copy-start = (bf16[256,384]{1,0:T(8,128)(2,1)S(1)}, bf16[256,384]{1,0:T(8,128)(2,1)}, u32[]{:S(2)}) copy-start(bf16[256,384]{1,0:T(8,128)(2,1)} %param.10) | copy-start | bytes 589828
  13.1 19.1 %copy-start.1 = (bf16[384]{0:T(512)(128)(2,1)S(1)}, bf16[384]{0:T(512)(128)(2,1)}, u32[]{:S(2)}) copy-start(bf16[384]{0:T(512)(128)(2,1)} %param.17) | copy-start | bytes 2308
  13.1 19.3 %copy-start.3 = (s32[2]{0:T(128)S(1)}, s32[2]{0:T(128)}, u32[]{:S(2)}) copy-start(s32[2]{0:T(128)} %param.14) | copy-start | bytes 28
  13.1 19.3 %copy-start.2 = (s32[2,64]{1,0:T(2,128)S(1)}, s32[2,64]{1,0:T(2,128)}, u32[]{:S(2)}) copy-start(s32[2,64]{1,0:T(2,128)} %param.13) | copy-start | bytes 1540
  13.1 171.8 %all-to-all-start = ((bf16[32,8,8,384]{3,2,1,0:T(8,128)(2,1)}), bf16[32,8,8,384]{3,2,1,0:T(8,128)(2,1)S(1)}, u32[]{:S(2)}, u32[]{:S(2)}) async-start(bf16[32,8,8,384]{3,2,1,0:T(8,128)(2,1)} %stack.2), calls=%async_computation | async-start | bytes 3145728 | tf_op jit(solution)/shard_map/all_to_all | solution.py:68
Sparse Core Ops, SparseCore 0:
  10.3 172.3 all-gather.7
  185.6 183.8 all-gather.3
  372.4 182.6 all-gather.5
